TPU v7x, 32 devices: a whole 2x2x4 slice. The times are simulated.
32 devices in a mesh: section: 2 (over x), batch: 16 (over z, y, core).
Axes of the slice: x: 2, y: 2, z: 4, core: 2. Of those that a mesh axis runs over, the one named last changes fastest.
Arguments:
- tokens: bfloat16 [2, 16, 1024, 384], P(None, 'batch'), may hold values from -6 to 6
- segments: int32 [2, 16, 1024], P(None, 'batch'), may hold values from 0 to 23, never falling along the last dimension, each value on 1 to 64 neighbouring positions
- cotangent: bfloat16 [2, 16, 1024, 384], P(None, 'batch'), may hold values from -6 to 6
- w_qkv: bfloat16 [2, 384, 1152], P('section'), may hold values from -0.3125 to 0.3125
- b_qkv: bfloat16 [2, 1152], P('section'), may hold values from -1.796875 to 1.796875
- w_out: bfloat16 [2, 384, 384], P('section'), may hold values from -0.875 to 0.875
- b_out: bfloat16 [2, 384], P('section'), may hold values from -3 to 3
- norm1_gain: bfloat16 [2, 384], P('section'), may hold values from 0.25 to 1.75
- norm1_bias: bfloat16 [2, 384], P('section'), may hold values from -1.796875 to 1.796875
- w_up: bfloat16 [2, 384, 1536], P('section'), may hold values from -0.3125 to 0.3125
- b_up: bfloat16 [2, 1536], P('section'), may hold values from -3 to 3
- w_down: bfloat16 [2, 1536, 384], P('section'), may hold values from -0.15625 to 0.15625
- b_down: bfloat16 [2, 384], P('section'), may hold values from -3 to 3
- norm2_gain: bfloat16 [2, 384], P('section'), may hold values from 0.25 to 1.75
- norm2_bias: bfloat16 [2, 384], P('section'), may hold values from -1.796875 to 1.796875
Outputs:
- layer_out: bfloat16 [2, 2, 16, 1024, 384], P('section', None, 'batch')
- layer_in_grad: bfloat16 [2, 2, 16, 1024, 384], P('section', None, 'batch')
- grad_w_qkv: float32 [2, 384, 1152], P('section')
- grad_b_qkv: float32 [2, 1152], P('section')
- grad_w_out: float32 [2, 384, 384], P('section')
- grad_b_out: float32 [2, 384], P('section')
- grad_norm1_gain: float32 [2, 384], P('section')
- grad_norm1_bias: float32 [2, 384], P('section')
- grad_w_up: float32 [2, 384, 1536], P('section')
- grad_b_up: float32 [2, 1536], P('section')
- grad_w_down: float32 [2, 1536, 384], P('section')
- grad_b_down: float32 [2, 384], P('section')
- grad_norm2_gain: float32 [2, 384], P('section')
- grad_norm2_bias: float32 [2, 384], P('section')
Inputs may be any that keep to these rules, and one draw needn't show every extreme that they name: `segments`: along each row the ids never fall; a document covers 1 to 64 consecutive positions.
All inputs are finite; a program needn't handle non-finite values.
Results may differ from a plain program's by a relative error of at most 0.015.
Values may be sent and summed in bfloat16 or wider, within the bound.
A program may use at most 320 MiB of HBM per device.

v0:
```python
import jax
import jax.numpy as jnp
from jax import lax
from jax.sharding import PartitionSpec as P

HEADS = 6
HEAD_DIM = 64
QBLOCK = 512
DOC_MOST = 64


NEG_LARGE = -1e30
NORM_EPS = 1e-12


def shifted(value, axis, steps):
    count = lax.axis_size(axis)
    first, last = (max(0, -steps), min(count, count - steps))
    return lax.ppermute(value, axis, [(source, source + steps) for source in range(first, last)])


def rows_t_times(left, right):
    return lax.dot_general(
        left, right, (((0,), (0,)), ((), ())), preferred_element_type=jnp.float32
    )


def times_t(left, right):
    return lax.dot_general(
        left, right, (((1,), (1,)), ((), ())), preferred_element_type=jnp.float32
    )


def rotary_tables(segment):
    length = segment.shape[-1]
    index = jnp.arange(length, dtype=jnp.int32)
    change = jnp.concatenate(
        [jnp.ones(segment.shape[:-1] + (1,), jnp.bool_), segment[..., 1:] != segment[..., :-1]],
        axis=-1,
    )
    start = lax.cummax(jnp.where(change, index, 0), axis=segment.ndim - 1)
    offset = (index - start).astype(jnp.float32).reshape(-1, 1)
    channel = jnp.arange(HEADS * HEAD_DIM, dtype=jnp.int32)
    pair_rank = (channel % HEAD_DIM // 2).astype(jnp.float32)
    freq = jnp.power(jnp.float32(10000.0), -2.0 * pair_rank / HEAD_DIM)
    angle = offset * freq
    signed = jnp.where(channel % 2 == 0, -1.0, 1.0).astype(jnp.float32)
    return (jnp.cos(angle), jnp.sin(angle) * signed)


def partner(value):
    count = value.shape[0]
    return value.reshape(count, -1, 2)[:, :, ::-1].reshape(count, -1)


def turn(value, cosine, sine_signed):
    return value * cosine + partner(value) * sine_signed


def turn_back(grad, cosine, sine_signed):
    return grad * cosine + partner(grad * sine_signed)


def standard(value):
    centre = jnp.mean(value, axis=-1, keepdims=True)
    centred = value - centre
    spread = jnp.mean(centred * centred, axis=-1, keepdims=True)
    scaling = lax.rsqrt(spread + NORM_EPS)
    return (centred * scaling, scaling)


def norm_back(grad, normed, scaling, gain):
    weighted = grad * gain
    gain_grad = jnp.sum(grad * normed, axis=0)
    bias_grad = jnp.sum(grad, axis=0)
    adjusted = (
        weighted
        - jnp.mean(weighted, axis=-1, keepdims=True)
        - normed * jnp.mean(weighted * normed, axis=-1, keepdims=True)
    )
    return (gain_grad, bias_grad, scaling * adjusted)


def gelu_slope(upward):
    normal_cdf = 0.5 * (1.0 + jax.scipy.special.erf(upward * 0.7071067811865476))
    density = jnp.exp(-0.5 * upward * upward) * 0.3989422804014327
    return normal_cdf + upward * density


def key_window(length):
    return min(length, QBLOCK + 2 * DOC_MOST)


def window_start(block_start, length, window):
    return jnp.clip(block_start - DOC_MOST, 0, length - window)


def attention(queries, keys_rot, values, segment):
    row_count, length = segment.shape
    blocks = length // QBLOCK
    window = key_window(length)
    scale = HEAD_DIM ** (-0.5)
    q_heads = queries.reshape(row_count, blocks, QBLOCK, HEADS, HEAD_DIM)
    k_heads = keys_rot.reshape(row_count, length, HEADS, HEAD_DIM)
    v_heads = values.reshape(row_count, length, HEADS, HEAD_DIM)
    seg_blocks = segment.reshape(row_count, blocks, QBLOCK)
    block_starts = jnp.arange(blocks, dtype=jnp.int32) * QBLOCK

    def one_row(item):
        q_row, k_row, v_row, seg_row, segq_row = item

        def one_block(block):
            q_block, seg_block, block_start = block
            first = window_start(block_start, length, window)
            k_win = lax.dynamic_slice_in_dim(k_row, first, window, 0)
            v_win = lax.dynamic_slice_in_dim(v_row, first, window, 0)
            seg_win = lax.dynamic_slice_in_dim(seg_row, first, window, 0)
            scores = (
                jnp.einsum("qhd,khd->hqk", q_block, k_win, preferred_element_type=jnp.float32)
                * scale
            )
            same = seg_block[:, None] == seg_win[None, :]
            scores = jnp.where(same[None], scores, NEG_LARGE)
            row_max = jnp.max(scores, axis=-1, keepdims=True)
            raised = jnp.exp(scores - row_max)
            summed = jnp.sum(raised, axis=-1, keepdims=True)
            attn_low = (raised / summed).astype(jnp.bfloat16)
            context = jnp.einsum(
                "hqk,khd->qhd", attn_low, v_win, preferred_element_type=jnp.float32
            ).astype(jnp.bfloat16)
            return (context, (row_max + jnp.log(summed))[..., 0])

        return lax.map(one_block, (q_row, segq_row, block_starts))

    context, log_total = lax.map(one_row, (q_heads, k_heads, v_heads, segment, seg_blocks))
    return (context.reshape(-1, HEADS * HEAD_DIM), log_total)


def attention_back(queries, keys_rot, values, d_context, log_total, segment):
    row_count, length = segment.shape
    blocks = length // QBLOCK
    window = key_window(length)
    scale = HEAD_DIM ** (-0.5)
    q_heads = queries.reshape(row_count, blocks, QBLOCK, HEADS, HEAD_DIM)
    k_heads = keys_rot.reshape(row_count, length, HEADS, HEAD_DIM)
    v_heads = values.reshape(row_count, length, HEADS, HEAD_DIM)
    dc_heads = d_context.reshape(row_count, blocks, QBLOCK, HEADS, HEAD_DIM)
    seg_blocks = segment.reshape(row_count, blocks, QBLOCK)
    block_starts = jnp.arange(blocks, dtype=jnp.int32) * QBLOCK

    def one_row(item):
        q_row, k_row, v_row, dc_row, total_row, seg_row, segq_row = item

        def one_block(carry, block):
            key_acc, value_acc = carry
            q_block, dc_block, total_block, seg_block, block_start = block
            first = window_start(block_start, length, window)
            k_win = lax.dynamic_slice_in_dim(k_row, first, window, 0)
            v_win = lax.dynamic_slice_in_dim(v_row, first, window, 0)
            seg_win = lax.dynamic_slice_in_dim(seg_row, first, window, 0)
            scores = (
                jnp.einsum("qhd,khd->hqk", q_block, k_win, preferred_element_type=jnp.float32)
                * scale
            )
            same = seg_block[:, None] == seg_win[None, :]
            scores = jnp.where(same[None], scores, NEG_LARGE)
            attn_probs = jnp.exp(scores - total_block[..., None])
            value_part = jnp.einsum(
                "hqk,qhd->khd",
                attn_probs.astype(jnp.bfloat16),
                dc_block,
                preferred_element_type=jnp.float32,
            )
            d_attn = jnp.einsum("qhd,khd->hqk", dc_block, v_win, preferred_element_type=jnp.float32)
            d_score = (
                attn_probs * (d_attn - jnp.sum(attn_probs * d_attn, axis=-1, keepdims=True))
            ).astype(jnp.bfloat16)
            d_query = (
                jnp.einsum("hqk,khd->qhd", d_score, k_win, preferred_element_type=jnp.float32)
                * scale
            )
            key_part = (
                jnp.einsum("hqk,qhd->khd", d_score, q_block, preferred_element_type=jnp.float32)
                * scale
            )
            key_acc = lax.dynamic_update_slice_in_dim(
                key_acc, lax.dynamic_slice_in_dim(key_acc, first, window, 0) + key_part, first, 0
            )
            value_acc = lax.dynamic_update_slice_in_dim(
                value_acc,
                lax.dynamic_slice_in_dim(value_acc, first, window, 0) + value_part,
                first,
                0,
            )
            return ((key_acc, value_acc), d_query)

        empty = jnp.zeros((length, HEADS, HEAD_DIM), jnp.float32)
        (d_key, d_value), d_query = lax.scan(
            one_block, (empty, empty), (q_row, dc_row, total_row, segq_row, block_starts)
        )
        return (d_query, d_key, d_value)

    d_query, d_key, d_value = lax.map(
        one_row, (q_heads, k_heads, v_heads, dc_heads, log_total, segment, seg_blocks)
    )
    width = HEADS * HEAD_DIM
    return (d_query.reshape(-1, width), d_key.reshape(-1, width), d_value.reshape(-1, width))


def forward_layer(params, entering, segment):
    (
        w_qkv,
        b_qkv,
        w_out,
        b_out,
        gain_one,
        bias_one,
        w_up,
        b_up,
        w_down,
        b_down,
        gain_two,
        bias_two,
    ) = params
    width = entering.shape[-1]
    flat_rows = entering.reshape(-1, width)
    cosine, sine_signed = rotary_tables(segment)
    projected = jnp.dot(flat_rows, w_qkv, preferred_element_type=jnp.float32) + b_qkv
    queries = turn(projected[:, :width], cosine, sine_signed).astype(jnp.bfloat16)
    keys_rot = turn(projected[:, width : 2 * width], cosine, sine_signed).astype(jnp.bfloat16)
    values = projected[:, 2 * width :].astype(jnp.bfloat16)
    context, log_total = attention(queries, keys_rot, values, segment)
    mixed = jnp.dot(context, w_out, preferred_element_type=jnp.float32) + b_out
    hat_one, scale_one = standard(flat_rows.astype(jnp.float32) + mixed)
    hidden = hat_one * gain_one + bias_one
    hidden_low = hidden.astype(jnp.bfloat16)
    upward = jnp.dot(hidden_low, w_up, preferred_element_type=jnp.float32) + b_up
    active = jax.nn.gelu(upward, approximate=False).astype(jnp.bfloat16)
    downward = jnp.dot(active, w_down, preferred_element_type=jnp.float32) + b_down
    hat_two, scale_two = standard(hidden + downward)
    leaving = (hat_two * gain_two + bias_two).astype(jnp.bfloat16).reshape(entering.shape)
    return (
        leaving,
        (
            queries,
            keys_rot,
            values,
            context,
            log_total,
            hat_one,
            scale_one,
            hidden_low,
            upward,
            active,
            hat_two,
            scale_two,
        ),
    )


def empty_forward(entering, segment, ff_width):
    row_count, length = segment.shape
    count = row_count * length
    width = entering.shape[-1]
    blocks = length // QBLOCK
    wide_low = jnp.zeros((count, width), jnp.bfloat16)
    wide_full = jnp.zeros((count, width), jnp.float32)
    column = jnp.zeros((count, 1), jnp.float32)
    log_total = jnp.zeros((row_count, blocks, HEADS, QBLOCK), jnp.float32)
    upward = jnp.zeros((count, ff_width), jnp.float32)
    active = jnp.zeros((count, ff_width), jnp.bfloat16)
    leaving = jnp.zeros(entering.shape, jnp.bfloat16)
    return (
        leaving,
        (
            wide_low,
            wide_low,
            wide_low,
            wide_low,
            log_total,
            wide_full,
            column,
            wide_low,
            upward,
            active,
            wide_full,
            column,
        ),
    )


def backward_layer(params, entering, segment, kept, arriving):
    (
        w_qkv,
        b_qkv,
        w_out,
        b_out,
        gain_one,
        bias_one,
        w_up,
        b_up,
        w_down,
        b_down,
        gain_two,
        bias_two,
    ) = params
    (
        queries,
        keys_rot,
        values,
        context,
        log_total,
        hat_one,
        scale_one,
        hidden_low,
        upward,
        active,
        hat_two,
        scale_two,
    ) = kept
    width = entering.shape[-1]
    flat_rows = entering.reshape(-1, width)
    grad_out = arriving.reshape(-1, width).astype(jnp.float32)
    g_gain_two, g_bias_two, back_two = norm_back(grad_out, hat_two, scale_two, gain_two)
    d_down = back_two.astype(jnp.bfloat16)
    g_b_down = jnp.sum(d_down.astype(jnp.float32), axis=0)
    g_w_down = rows_t_times(active, d_down)
    d_up = (times_t(d_down, w_down) * gelu_slope(upward)).astype(jnp.bfloat16)
    g_b_up = jnp.sum(d_up.astype(jnp.float32), axis=0)
    g_w_up = rows_t_times(hidden_low, d_up)
    d_hidden = back_two + times_t(d_up, w_up)
    g_gain_one, g_bias_one, back_one = norm_back(d_hidden, hat_one, scale_one, gain_one)
    d_mixed = back_one.astype(jnp.bfloat16)
    g_b_out = jnp.sum(d_mixed.astype(jnp.float32), axis=0)
    g_w_out = rows_t_times(context, d_mixed)
    d_context = times_t(d_mixed, w_out).astype(jnp.bfloat16)
    d_query, d_key, d_value = attention_back(
        queries, keys_rot, values, d_context, log_total, segment
    )
    cosine, sine_signed = rotary_tables(segment)
    d_proj = jnp.concatenate(
        [turn_back(d_query, cosine, sine_signed), turn_back(d_key, cosine, sine_signed), d_value],
        axis=1,
    ).astype(jnp.bfloat16)
    g_b_qkv = jnp.sum(d_proj.astype(jnp.float32), axis=0)
    g_w_qkv = rows_t_times(flat_rows, d_proj)
    d_entering = (back_one + times_t(d_proj, w_qkv)).astype(jnp.bfloat16).reshape(entering.shape)
    return (
        d_entering,
        (
            g_w_qkv,
            g_b_qkv,
            g_w_out,
            g_b_out,
            g_gain_one,
            g_bias_one,
            g_w_up,
            g_b_up,
            g_w_down,
            g_b_down,
            g_gain_two,
            g_bias_two,
        ),
    )


def empty_backward(params, entering):
    return (
        jnp.zeros(entering.shape, jnp.bfloat16),
        tuple((jnp.zeros(p.shape, jnp.float32) for p in params)),
    )


def write_slot(buffer, piece, slot_index, is_live):
    previous = lax.dynamic_index_in_dim(buffer, slot_index, 0, keepdims=False)
    return lax.dynamic_update_index_in_dim(
        buffer, jnp.where(is_live, piece, previous), slot_index, 0
    )


def body(
    tokens,
    segments,
    cotangent,
    w_qkv,
    b_qkv,
    w_out,
    b_out,
    norm1_gain,
    norm1_bias,
    w_up,
    b_up,
    w_down,
    b_down,
    norm2_gain,
    norm2_bias,
):
    params = tuple(
        (
            w[0]
            for w in (
                w_qkv,
                b_qkv,
                w_out,
                b_out,
                norm1_gain,
                norm1_bias,
                w_up,
                b_up,
                w_down,
                b_down,
                norm2_gain,
                norm2_bias,
            )
        )
    )
    ff_width = w_up.shape[2]
    section_index = lax.axis_index("section")
    on_first = section_index == 0
    micro_count = tokens.shape[0]
    layer_out = jnp.zeros(tokens.shape, jnp.bfloat16)
    layer_in_grad = jnp.zeros(tokens.shape, jnp.bfloat16)
    received = jnp.zeros(tokens.shape[1:], jnp.bfloat16)
    entries = []
    for moment in range(micro_count + 1):
        micro_index = moment - section_index
        is_live = (micro_index >= 0) & (micro_index < micro_count)
        slot_index = jnp.clip(micro_index, 0, micro_count - 1)
        own_input = tokens[min(moment, micro_count - 1)]
        entering = jnp.where(on_first, own_input, received)
        segment = lax.dynamic_index_in_dim(segments, slot_index, 0, keepdims=False)

        def run_forward(entering=entering, segment=segment):
            return forward_layer(params, entering, segment)

        def skip_forward(entering=entering, segment=segment):
            return empty_forward(entering, segment, ff_width)

        leaving, kept = lax.cond(is_live, run_forward, skip_forward)
        entries.append((entering, segment, kept))
        layer_out = write_slot(layer_out, leaving, slot_index, is_live)
        if moment < micro_count:
            received = shifted(leaving, "section", 1)
    totals = tuple((jnp.zeros(p.shape, jnp.float32) for p in params))
    back_in = jnp.zeros(tokens.shape[1:], jnp.bfloat16)
    for moment in range(micro_count + 1):
        micro_index = moment - 1 + section_index
        is_live = (micro_index >= 0) & (micro_index < micro_count)
        slot_index = jnp.clip(micro_index, 0, micro_count - 1)
        before = entries[max(moment - 1, 0)]
        after = entries[min(moment + 1, micro_count)]
        entering, segment, kept = jax.tree.map(
            lambda a, b: jnp.where(on_first, a, b), before, after
        )
        arriving = jnp.where(on_first, back_in, cotangent[min(moment, micro_count - 1)])

        def run_backward(entering=entering, segment=segment, kept=kept, arriving=arriving):
            return backward_layer(params, entering, segment, kept, arriving)

        def skip_backward(entering=entering, segment=segment, kept=kept, arriving=arriving):
            return empty_backward(params, entering)

        d_entering, grads = lax.cond(is_live, run_backward, skip_backward)
        layer_in_grad = write_slot(layer_in_grad, d_entering, slot_index, is_live)
        totals = tuple((a + b for a, b in zip(totals, grads)))
        if moment < micro_count:
            back_in = shifted(d_entering, "section", -1)
    final = lax.psum(
        (
            totals[0],
            totals[1],
            totals[2],
            totals[3],
            totals[4],
            totals[5],
            totals[6],
            totals[7],
            totals[8],
            totals[9],
            totals[10],
            totals[11],
        ),
        "batch",
    )
    return (
        layer_out[None],
        layer_in_grad[None],
        final[0][None],
        final[1][None],
        final[2][None],
        final[3][None],
        final[4][None],
        final[5][None],
        final[6][None],
        final[7][None],
        final[8][None],
        final[9][None],
        final[10][None],
        final[11][None],
    )


def solution(mesh):
    in_specs = (
        P(None, "batch", None, None),
        P(None, "batch", None),
        P(None, "batch", None, None),
        P("section", None, None),
        P("section", None),
        P("section", None, None),
        P("section", None),
        P("section", None),
        P("section", None),
        P("section", None, None),
        P("section", None),
        P("section", None, None),
        P("section", None),
        P("section", None),
        P("section", None),
    )
    out_specs = (
        P("section", None, "batch", None, None),
        P("section", None, "batch", None, None),
        P("section", None, None),
        P("section", None),
        P("section", None, None),
        P("section", None),
        P("section", None),
        P("section", None),
        P("section", None, None),
        P("section", None),
        P("section", None, None),
        P("section", None),
        P("section", None),
        P("section", None),
    )
    return jax.shard_map(body, mesh=mesh, in_specs=in_specs, out_specs=out_specs, check_vma=False)
```

profile of v0, /device:TPU:0, one launch (start us, length us, event | category | flops | bytes accessed | tf_op | source)
XLA Modules:
  0.0 1316.9 jit_solution(1449218410256763336)
XLA Ops:
  16.2 96.8 %conditional.6 = (bf16[1024,384]{1,0:T(8,128)(2,1)S(1)}, bf16[1024,384]{1,0:T(8,128)(2,1)S(1)}, bf16[1024,384]{1,0:T(8,128)(2,1)}, bf16[1024,384]{0,1:T(8,128)(2...) conditional(s32[]{:T(128)} %convert_element_type.453, ...), branch_computations={%region_0.1_spmd, %region_1.12_spmd} | conditional | flops 4270218240 | bytes 192266624 | solution.py:439
  23.2 5.7 rev.25
  35.4 5.7 rev.24
  43.8 9.1 fusion.159
  60.6 19.1 %while.144 = (s32[]{:T(128)}, bf16[2,512,6,64]{1,3,2,0:T(8,128)(2,1)}, f32[2,6,512]{2,1,0:T(8,128)S(1)}, s32[2]{0:T(128)S(1)}, bf16[1024,6,64]{0,2,1:T(8,128)(2,...) while((s32[]{:T(128)}, ...), condition=%wide.region_7.7_spmd, body=%wide.region_4.6_spmd.sunk | while | flops 527430656 | bytes 36243236 | solution.py:133
  86.4 17.9 %fusion.146 = (bf16[1024,1536]{1,0:T(8,128)(2,1)}, f32[1024,1536]{1,0:T(8,128)}) fusion(f32[1536]{0:T(1024)S(1)} %convert_element_type.349, bf16[1024,384]{0,1:T(8,128)(2,1)} %get-tuple-element.3588, bf16[384,1536]{1,0:T(8,128)(2,1)S(1)} %copy-done.45), kind=kOutput, calls=%fused_computation.174 | convolution fusion | flops 1311768576 | bytes 11409408 | tf_op jit(solution)/shard_map/cond/branch_1_fun/dot_general | solution.py:237
  115.4 17.1 %collective-permute-done = bf16[1,1024,384]{2,1,0:T(8,128)(2,1)} collective-permute-done((bf16[1,1024,384]{2,1,0:T(8,128)(2,1)}, bf16[1,1024,384]{2,1,0:T(8,128)(2,1)}, u32[]{:S(2)}, u32[]{:S(2)}) %collective-permute-start) | collective-permute-done | bytes 786464 | tf_op jit(solution)/shard_map/ppermute | solution.py:19
  134.6 95.5 %conditional.7 = (bf16[1024,384]{1,0:T(8,128)(2,1)}, bf16[1024,384]{1,0:T(8,128)(2,1)}, bf16[1024,384]{1,0:T(8,128)(2,1)}, bf16[1024,384]{0,1:T(8,128)(2,1)}, f3...) conditional(s32[]{:T(128)} %convert_element_type.454, ...), branch_computations={%region_12.13_spmd, %region_13.24_spmd} | conditional | flops 4270218240 | bytes 181764384 | solution.py:439
  140.1 5.7 rev.27
  152.3 5.7 rev.26
  160.7 9.6 fusion.197
  178.8 18.8 %while.145 = (s32[]{:T(128)}, bf16[2,512,6,64]{1,3,2,0:T(8,128)(2,1)}, f32[2,6,512]{2,1,0:T(8,128)S(1)}, s32[2]{0:T(128)S(1)}, bf16[1024,6,64]{0,2,1:T(8,128)(2,...) while((s32[]{:T(128)}, ...), condition=%wide.region_19.19_spmd, body=%wide.region_16.18_spmd.sunk | while | flops 527430656 | bytes 33097480 | solution.py:133
  204.3 18.2 %fusion.184 = (bf16[1024,1536]{1,0:T(8,128)(2,1)}, f32[1024,1536]{1,0:T(8,128)}) fusion(f32[1536]{0:T(1024)S(1)} %convert_element_type.368, bf16[1024,384]{0,1:T(8,128)(2,1)} %get-tuple-element.3614, bf16[384,1536]{1,0:T(8,128)(2,1)S(1)} %copy-done.46), kind=kOutput, calls=%fused_computation.254 | convolution fusion | flops 1311768576 | bytes 11409408 | tf_op jit(solution)/shard_map/cond/branch_1_fun/dot_general | solution.py:237
  230.2 5.7 collective-permute-start.1
  239.5 17.8 %conditional.9 = (bf16[1,1024,384]{2,1,0:T(8,128)(2,1)}, f32[384,1152]{1,0:T(8,128)}, f32[1152]{0:T(1024)S(1)}, f32[384,384]{1,0:T(8,128)}, f32[384]{0:T(512)S(1...) conditional(s32[]{:T(128)} %convert_element_type.456, ...), branch_computations={%region_36.37_spmd, %region_37.55_spmd} | conditional | flops 8605775872 | bytes 402297248 | solution.py:463
  263.2 16.9 %conditional.8 = (bf16[1024,384]{1,0:T(8,128)(2,1)S(1)}, bf16[1024,384]{1,0:T(8,128)(2,1)}, bf16[1024,384]{1,0:T(8,128)(2,1)}, bf16[1024,384]{0,1:T(8,128)(2,1)}...) conditional(s32[]{:T(128)} %convert_element_type.455, ...), branch_computations={%region_24.25_spmd, %region_25.36_spmd} | conditional | flops 4270218240 | bytes 178619200 | solution.py:439
  280.1 222.1 %collective-permute-done.2 = bf16[1,1024,384]{2,1,0:T(8,128)(2,1)} collective-permute-done((bf16[1,1024,384]{2,1,0:T(8,128)(2,1)}, bf16[1,1024,384]{2,1,0:T(8,128)(2,1)}, u32[]{:S(2)}, u32[]{:S(2)}) %collective-permute-start.2) | collective-permute-done | bytes 786464 | tf_op jit(solution)/shard_map/ppermute | solution.py:19
  502.2 244.0 %conditional.10 = (bf16[1,1024,384]{2,1,0:T(8,128)(2,1)}, f32[384,1152]{1,0:T(8,128)}, f32[1152]{0:T(1024)S(1)}, f32[384,384]{1,0:T(8,128)}, f32[384]{0:T(512)S(...) conditional(s32[]{:T(128)} %convert_element_type.457, ...), branch_computations={%region_55.56_spmd, %region_56.74_spmd} | conditional | flops 8605775872 | bytes 411734496 | solution.py:463
  519.0 8.5 convert_reduce_fusion.5
  552.3 94.6 %while.148 = (s32[]{:T(128)}, f32[1024,6,64]{0,2,1:T(8,128)S(1)}, f32[1024,6,64]{0,2,1:T(8,128)}, f32[2,512,6,64]{1,0,3,2:T(2,128)}, s32[2]{0:T(128)S(1)}, /*ind...) while((s32[]{:T(128)}, f32[1024,6,64]{0,2,1:T(8,128)S(1)}, ...), condition=%wide.region_63.63_spmd, body=%wide.region_61.62_spmd.sunk | while | flops 1289040896 | bytes 122425648 | solution.py:198
  556.6 5.4 multiply_reduce_fusion.22
  570.6 6.0 fusion.526
  585.8 14.9 %dynamic_update_slice.186 = f32[2,512,6,64]{1,0,3,2:T(2,128)} dynamic-update-slice(f32[2,512,6,64]{1,0,3,2:T(2,128)} %get-tuple-element.3369, f32[1,512,6,64]{1,0,3,2:T(1,128)S(1)} %copy.339, s32[]{:T(128)S(6)} %copy.363, s32[]{:T(128)} %constant.1120.clone..sunk, s32[]{:T(128)} %constant.1120.clone..sunk, s32[]{:T(128)} %constant.1120.clone..sunk) | dynamic-update-slice | bytes 1572868 | tf_op jit(solution)/shard_map/cond/branch_1_fun/while/body/eval_jaxpr/while/body/jit(dynamic_update_index_in_dim)/dynamic_update_slice | solution.py:198
  604.8 5.3 multiply_reduce_fusion.22
  617.7 5.8 fusion.526
  632.0 14.9 %dynamic_update_slice.186 = f32[2,512,6,64]{1,0,3,2:T(2,128)} dynamic-update-slice(f32[2,512,6,64]{1,0,3,2:T(2,128)} %get-tuple-element.3369, f32[1,512,6,64]{1,0,3,2:T(1,128)S(1)} %copy.339, s32[]{:T(128)S(6)} %copy.363, s32[]{:T(128)} %constant.1120.clone..sunk, s32[]{:T(128)} %constant.1120.clone..sunk, s32[]{:T(128)} %constant.1120.clone..sunk) | dynamic-update-slice | bytes 1572868 | tf_op jit(solution)/shard_map/cond/branch_1_fun/while/body/eval_jaxpr/while/body/jit(dynamic_update_index_in_dim)/dynamic_update_slice | solution.py:198
  657.2 24.2 %fusion.323 = (f32[1024,192,2]{0,2,1:T(2,128)}, f32[1024,192,2]{0,2,1:T(2,128)}) fusion(f32[1024,192,2]{0,2,1:T(2,128)} %reshape.1631, f32[192,2]{1,0:T(8,128)S(1)} %copy.236, f32[192,2]{1,0:T(8,128)S(1)} %copy.235, f32[1024]{0:T(1024)S(1)} %fusion.332, f32[1024,192,2]{0,2,1:T(2,128)} %reshape.1634), kind=kLoop, calls=%fused_computation.543 | loop fusion | flops 1572864 | bytes 6298624 | tf_op jit(solution)/shard_map/cond/branch_1_fun/mul | solution.py:61
  681.4 10.7 rev.32
  698.1 10.7 rev.33
  712.0 7.2 add_convert_fusion.6
  740.2 6.1 fusion.308
  747.6 137.9 %collective-permute-done.3 = bf16[1,1024,384]{2,1,0:T(8,128)(2,1)S(1)} collective-permute-done((bf16[1,1024,384]{2,1,0:T(8,128)(2,1)}, bf16[1,1024,384]{2,1,0:T(8,128)(2,1)S(1)}, u32[]{:S(2)}, u32[]{:S(2)}) %collective-permute-start.3) | collective-permute-done | bytes 786464 | tf_op jit(solution)/shard_map/ppermute | solution.py:19
  885.6 247.9 %conditional.11 = (bf16[1,1024,384]{2,1,0:T(8,128)(2,1)}, f32[384,1152]{1,0:T(8,128)}, f32[1152]{0:T(1024)}, f32[384,384]{1,0:T(8,128)}, f32[384]{0:T(512)}, /*i...) conditional(s32[]{:T(128)} %convert_element_type.458, ...), branch_computations={%region_74.75_spmd, %region_75.93_spmd} | conditional | flops 8605775872 | bytes 401920480 | solution.py:463
  904.1 9.1 convert_reduce_fusion.10
  939.0 94.7 %while.149 = (s32[]{:T(128)}, f32[1024,6,64]{0,2,1:T(8,128)S(1)}, f32[1024,6,64]{0,2,1:T(8,128)}, f32[2,512,6,64]{1,0,3,2:T(2,128)}, s32[2]{0:T(128)S(1)}, /*ind...) while((s32[]{:T(128)}, f32[1024,6,64]{0,2,1:T(8,128)S(1)}, ...), condition=%wide.region_82.82_spmd, body=%wide.region_80.81_spmd.sunk | while | flops 1289040896 | bytes 122425648 | solution.py:198
  943.5 5.4 multiply_reduce_fusion.21
  957.5 5.9 fusion.514
  972.6 14.9 %dynamic_update_slice.183 = f32[2,512,6,64]{1,0,3,2:T(2,128)} dynamic-update-slice(f32[2,512,6,64]{1,0,3,2:T(2,128)} %get-tuple-element.3318, f32[1,512,6,64]{1,0,3,2:T(1,128)S(1)} %copy.338, s32[]{:T(128)S(6)} %copy.348, s32[]{:T(128)} %constant.1151.clone..sunk, s32[]{:T(128)} %constant.1151.clone..sunk, s32[]{:T(128)} %constant.1151.clone..sunk) | dynamic-update-slice | bytes 1572868 | tf_op jit(solution)/shard_map/cond/branch_1_fun/while/body/eval_jaxpr/while/body/jit(dynamic_update_index_in_dim)/dynamic_update_slice | solution.py:198
  991.5 5.3 multiply_reduce_fusion.21
  1004.4 5.8 fusion.514
  1018.7 14.9 %dynamic_update_slice.183 = f32[2,512,6,64]{1,0,3,2:T(2,128)} dynamic-update-slice(f32[2,512,6,64]{1,0,3,2:T(2,128)} %get-tuple-element.3318, f32[1,512,6,64]{1,0,3,2:T(1,128)S(1)} %copy.338, s32[]{:T(128)S(6)} %copy.348, s32[]{:T(128)} %constant.1151.clone..sunk, s32[]{:T(128)} %constant.1151.clone..sunk, s32[]{:T(128)} %constant.1151.clone..sunk) | dynamic-update-slice | bytes 1572868 | tf_op jit(solution)/shard_map/cond/branch_1_fun/while/body/eval_jaxpr/while/body/jit(dynamic_update_index_in_dim)/dynamic_update_slice | solution.py:198
  1043.6 24.2 %fusion.367 = (f32[1024,192,2]{0,2,1:T(2,128)}, f32[1024,192,2]{0,2,1:T(2,128)}) fusion(f32[1024,192,2]{0,2,1:T(2,128)} %reshape.1644, f32[192,2]{1,0:T(8,128)S(1)} %copy.246, f32[192,2]{1,0:T(8,128)S(1)} %copy.245, f32[1024]{0:T(1024)S(1)} %fusion.376, f32[1024,192,2]{0,2,1:T(2,128)} %reshape.1647), kind=kLoop, calls=%fused_computation.634 | loop fusion | flops 1572864 | bytes 6298624 | tf_op jit(solution)/shard_map/cond/branch_1_fun/mul | solution.py:61
  1067.8 10.7 rev.34
  1084.6 10.7 rev.35
  1098.5 7.2 add_convert_fusion.8
  1127.1 6.2 fusion.352
  1160.3 63.4 %all-reduce = (f32[1,1152]{1,0:T(1,128)}, f32[1,384]{1,0:T(1,128)}, f32[1,384]{1,0:T(1,128)}, f32[1,384]{1,0:T(1,128)}, f32[1,1536]{1,0:T(1,128)}, /*index=5*/f3...) all-reduce(f32[1,1152]{1,0:T(1,128)S(1)} %broadcast_in_dim.412, ...), channel_id=1, replica_groups=mesh['section'=2,'batch'=16] {'batch'}, use_global_device_ids=true, to_apply=%region_94.95 | all-reduce | flops 4992 | bytes 39936 | tf_op jit(solution)/shard_map/psum | solution.py:468
  1225.2 76.9 %all-reduce.4.cloned.1.call-done = (f32[1,384,1152]{2,1,0:T(8,128)}, f32[1,384,384]{2,1,0:T(8,128)}, f32[1,384,1536]{2,1,0:T(8,128)}, f32[1,1536,384]{2,1,0:T(8,128)}) async-done(((f32[1,384,1152]{2,1,0:T(8,128)}, f32[1,384,384]{2,1,0:T(8,128)}, f32[1,384,1536]{2,1,0:T(8,128)}, f32[1,1536,384]{2,1,0:T(8,128)}), (f32[1,384,1152]{2,1,0:T(8,128)}, f32[1,384,384]{2,1,0:T(8,128)}, f32[1,384,1536]{2,1,0:T(8,128)}, ...) | async-done | bytes 7077904 | tf_op jit(solution)/shard_map/psum | solution.py:468
  (734 shorter events, 438.9 us)
Async XLA Ops:
  7.2 1294.9 %all-reduce.4.cloned.1.call-start = ((), (), s32[]{:S(2)}) async-start(), calls=%async_computation | async-start | bytes 14155776 | tf_op jit(solution)/shard_map/psum | solution.py:468
  8.0 125.8 %copy-start.146 = (bf16[1152]{0:T(1024)(128)(2,1)}, bf16[1152]{0:T(1024)(128)(2,1)S(1)}, u32[]{:S(2)}) copy-start(bf16[1152]{0:T(1024)(128)(2,1)S(1)} %reduce.21) | copy-start | bytes 6916
  8.7 125.1 %copy-start.160 = (bf16[384]{0:T(512)(128)(2,1)}, bf16[384]{0:T(512)(128)(2,1)S(1)}, u32[]{:S(2)}) copy-start(bf16[384]{0:T(512)(128)(2,1)S(1)} %reduce.22) | copy-start | bytes 2308
  10.1 123.7 %copy-start.162 = (bf16[384]{0:T(512)(128)(2,1)}, bf16[384]{0:T(512)(128)(2,1)S(1)}, u32[]{:S(2)}) copy-start(bf16[384]{0:T(512)(128)(2,1)S(1)} %reduce.24) | copy-start | bytes 2308
  10.8 123.0 %copy-start.148 = (bf16[1536]{0:T(1024)(128)(2,1)}, bf16[1536]{0:T(1024)(128)(2,1)S(1)}, u32[]{:S(2)}) copy-start(bf16[1536]{0:T(1024)(128)(2,1)S(1)} %reduce.25) | copy-start | bytes 9220
  11.5 122.3 %copy-start.164 = (bf16[384]{0:T(512)(128)(2,1)}, bf16[384]{0:T(512)(128)(2,1)S(1)}, u32[]{:S(2)}) copy-start(bf16[384]{0:T(512)(128)(2,1)S(1)} %reduce.26) | copy-start | bytes 2308
  12.9 120.9 %copy-start.166 = (bf16[384]{0:T(512)(128)(2,1)}, bf16[384]{0:T(512)(128)(2,1)S(1)}, u32[]{:S(2)}) copy-start(bf16[384]{0:T(512)(128)(2,1)S(1)} %reduce.28) | copy-start | bytes 2308
  85.1 19.2 %copy-start.132 = (f32[1024]{0:T(1024)}, f32[1024]{0:T(1024)S(1)}, u32[]{:S(2)}) copy-start(f32[1024]{0:T(1024)S(1)} %add_rsqrt_fusion.1) | copy-start | bytes 12292 | tf_op jit(solution)/shard_map/cond
  86.3 18.0 %copy-start.8 = (f32[1024,384]{0,1:T(8,128)}, f32[1024,384]{0,1:T(8,128)S(1)}, u32[]{:S(2)}) copy-start(f32[1024,384]{0,1:T(8,128)S(1)} %get-tuple-element.3586) | copy-start | bytes 4718596 | tf_op jit(solution)/shard_map/cond
  86.4 17.9 %copy-start.186 = (bf16[1536,384]{1,0:T(8,128)(2,1)S(1)}, bf16[1536,384]{1,0:T(8,128)(2,1)}, u32[]{:S(2)}) copy-start(bf16[1536,384]{1,0:T(8,128)(2,1)} %get-tuple-element.1334) | copy-start | bytes 3538948 | tf_op jit(solution)/shard_map/cond
  113.0 20.8 %copy-start.11 = (f32[1024,384]{0,1:T(8,128)}, f32[1024,384]{0,1:T(8,128)S(1)}, u32[]{:S(2)}) copy-start(f32[1024,384]{0,1:T(8,128)S(1)} %get-tuple-element.1664) | copy-start | bytes 4718596
  113.0 20.8 %copy-start.26 = (bf16[1024,384]{1,0:T(8,128)(2,1)}, bf16[1024,384]{1,0:T(8,128)(2,1)S(1)}, u32[]{:S(2)}) copy-start(bf16[1024,384]{1,0:T(8,128)(2,1)S(1)} %get-tuple-element.1670) | copy-start | bytes 2359300
  113.0 20.8 %copy-start.31 = (bf16[1024,384]{1,0:T(8,128)(2,1)}, bf16[1024,384]{1,0:T(8,128)(2,1)S(1)}, u32[]{:S(2)}) copy-start(bf16[1024,384]{1,0:T(8,128)(2,1)S(1)} %get-tuple-element.1674) | copy-start | bytes 2359300
  113.0 20.7 %copy-start.37 = (bf16[1,384,384]{2,1,0:T(8,128)(2,1)S(1)}, bf16[1,384,384]{2,1,0:T(8,128)(2,1)}, u32[]{:S(2)}) copy-start(bf16[1,384,384]{2,1,0:T(8,128)(2,1)} %param.44) | copy-start | bytes 884740
  113.0 20.7 %copy-start.118 = (s32[1,1024]{1,0:T(1,128)S(1)}, s32[1,1024]{1,0:T(1,128)}, u32[]{:S(2)}) copy-start(s32[1,1024]{1,0:T(1,128)} %get-tuple-element.2883) | copy-start | bytes 12292
  113.0 19.4 %collective-permute-start = (bf16[1,1024,384]{2,1,0:T(8,128)(2,1)}, bf16[1,1024,384]{2,1,0:T(8,128)(2,1)}, u32[]{:S(2)}, u32[]{:S(2)}) collective-permute-start(bf16[1,1024,384]{2,1,0:T(8,128)(2,1)} %get-tuple-element.2587), channel_id=1, source_target_pairs={{0,16},{1,17},{2,18},{3,19},{4,20},{5,21},{6,22},{7,23},{8,24},{9,... | collective-permute-start | bytes 2359304 | tf_op jit(solution)/shard_map/ppermute | solution.py:19
  115.4 18.4 %copy-start.192 = (bf16[1,384,1152]{2,1,0:T(8,128)(2,1)S(1)}, bf16[1,384,1152]{2,1,0:T(8,128)(2,1)}, u32[]{:S(2)}) copy-start(bf16[1,384,1152]{2,1,0:T(8,128)(2,1)} %param.42) | copy-start | bytes 2654212
  203.0 19.6 %copy-start.135 = (f32[1024]{0:T(1024)}, f32[1024]{0:T(1024)S(1)}, u32[]{:S(2)}) copy-start(f32[1024]{0:T(1024)S(1)} %add_rsqrt_fusion.3) | copy-start | bytes 12292 | tf_op jit(solution)/shard_map/cond
  204.1 18.4 %copy-start.14 = (f32[1024,384]{0,1:T(8,128)}, f32[1024,384]{0,1:T(8,128)S(1)}, u32[]{:S(2)}) copy-start(f32[1024,384]{0,1:T(8,128)S(1)} %get-tuple-element.3612) | copy-start | bytes 4718596 | tf_op jit(solution)/shard_map/cond
  204.3 18.3 %copy-start.187 = (bf16[1536,384]{1,0:T(8,128)(2,1)S(1)}, bf16[1536,384]{1,0:T(8,128)(2,1)}, u32[]{:S(2)}) copy-start(bf16[1536,384]{1,0:T(8,128)(2,1)} %get-tuple-element.1360) | copy-start | bytes 3538948 | tf_op jit(solution)/shard_map/cond
  230.1 9.3 copy-start.128
  230.1 9.3 copy-start.137
  230.1 9.3 copy-start.9
  230.1 9.2 copy-start.27
  230.2 30.9 %collective-permute-start.1 = (bf16[1,1024,384]{2,1,0:T(8,128)(2,1)}, bf16[1,1024,384]{2,1,0:T(8,128)(2,1)}, u32[]{:S(2)}, u32[]{:S(2)}) collective-permute-start(bf16[1,1024,384]{2,1,0:T(8,128)(2,1)} %get-tuple-element.2588), channel_id=1, source_target_pairs={{0,16},{1,17},{2,18},{3,19},{4,20},{5,21},{6,22},{7,23},{8,24},{9,... | collective-permute-start | bytes 2359304 | tf_op jit(solution)/shard_map/ppermute | solution.py:19
  257.4 244.7 %collective-permute-start.2 = (bf16[1,1024,384]{2,1,0:T(8,128)(2,1)}, bf16[1,1024,384]{2,1,0:T(8,128)(2,1)}, u32[]{:S(2)}, u32[]{:S(2)}) collective-permute-start(bf16[1,1024,384]{2,1,0:T(8,128)(2,1)} %get-tuple-element.1684), channel_id=1, source_target_pairs={{16,0},{17,1},{18,2},{19,3},{20,4},{21,5},{22,6},{23,7},{24,8},{25... | collective-permute-start | bytes 2359304 | tf_op jit(solution)/shard_map/ppermute | solution.py:19
  262.4 239.7 %copy-start.7 = (pred[1024,384]{1,0:T(32,128)(4,1)S(1)}, pred[1024,384]{1,0:T(32,128)(4,1)}, u32[]{:S(2)}) copy-start(pred[1024,384]{1,0:T(32,128)(4,1)} %copy-done.6) | copy-start | bytes 1179652
  262.4 239.7 %copy-start.10 = (f32[1024,384]{0,1:T(8,128)S(1)}, f32[1024,384]{0,1:T(8,128)}, u32[]{:S(2)}) copy-start(f32[1024,384]{0,1:T(8,128)} %get-tuple-element.1668) | copy-start | bytes 4718596
  262.4 239.7 %copy-start.122 = (s32[1,1024]{1,0:T(1,128)S(1)}, s32[1,1024]{1,0:T(1,128)}, u32[]{:S(2)}) copy-start(s32[1,1024]{1,0:T(1,128)} %copy-done.120) | copy-start | bytes 12292
  262.4 239.7 %copy-start.125 = (f32[1,2,6,512]{3,2,1,0:T(8,128)S(1)}, f32[1,2,6,512]{3,2,1,0:T(8,128)}, u32[]{:S(2)}) copy-start(f32[1,2,6,512]{3,2,1,0:T(8,128)} %get-tuple-element.1672) | copy-start | bytes 73732
  262.4 239.7 %copy-start.134 = (f32[1024,1]{0,1:T(1,128)S(1)}, f32[1024,1]{0,1:T(1,128)}, u32[]{:S(2)}) copy-start(f32[1024,1]{0,1:T(1,128)} %get-tuple-element.1660) | copy-start | bytes 12292
  262.4 239.7 %copy-start.144 = (pred[1024,1]{0,1:T(4,128)(4,1)S(1)}, pred[1024,1]{0,1:T(4,128)(4,1)}, u32[]{:S(2)}) copy-start(pred[1024,1]{0,1:T(4,128)(4,1)} %copy-done.143) | copy-start | bytes 3076
  262.5 239.7 %copy-start.151 = (pred[1,1024]{1,0:T(4,128)(4,1)S(1)}, pred[1,1024]{1,0:T(4,128)(4,1)}, u32[]{:S(2)}) copy-start(pred[1,1024]{1,0:T(4,128)(4,1)} %copy-done.150) | copy-start | bytes 3076
  280.1 222.2 %copy-start.34 = (bf16[1024,384]{1,0:T(8,128)(2,1)}, bf16[1024,384]{1,0:T(8,128)(2,1)S(1)}, u32[]{:S(2)}) copy-start(bf16[1024,384]{1,0:T(8,128)(2,1)S(1)} %get-tuple-element.1690) | copy-start | bytes 2359300
  280.1 222.2 %copy-start.141 = (f32[1024,1]{0,1:T(1,128)}, f32[1024,1]{0,1:T(1,128)S(1)}, u32[]{:S(2)}) copy-start(f32[1024,1]{0,1:T(1,128)S(1)} %get-tuple-element.1685) | copy-start | bytes 12292
  502.2 383.4 %copy-start.119 = (s32[1,1024]{1,0:T(1,128)S(1)}, s32[1,1024]{1,0:T(1,128)}, u32[]{:S(2)}) copy-start(s32[1,1024]{1,0:T(1,128)} %get-tuple-element.2883) | copy-start | bytes 12292
  502.2 383.4 %copy-start.129 = (f32[1,2,6,512]{3,2,1,0:T(8,128)S(1)}, f32[1,2,6,512]{3,2,1,0:T(8,128)}, u32[]{:S(2)}) copy-start(f32[1,2,6,512]{3,2,1,0:T(8,128)} %copy-done.128) | copy-start | bytes 73732
  502.2 383.4 %copy-start.138 = (f32[1024,1]{0,1:T(1,128)S(1)}, f32[1024,1]{0,1:T(1,128)}, u32[]{:S(2)}) copy-start(f32[1024,1]{0,1:T(1,128)} %copy-done.137) | copy-start | bytes 12292
  502.2 383.4 %copy-start.145 = (pred[1024,1]{0,1:T(4,128)(4,1)S(1)}, pred[1024,1]{0,1:T(4,128)(4,1)}, u32[]{:S(2)}) copy-start(pred[1024,1]{0,1:T(4,128)(4,1)} %copy-done.143) | copy-start | bytes 3076
  530.4 14.6 %copy-start.18 = (f32[1024,384]{1,0:T(8,128)}, f32[1024,384]{1,0:T(8,128)S(1)}, u32[]{:S(2)}) copy-start(f32[1024,384]{1,0:T(8,128)S(1)} %get-tuple-element.2776) | copy-start | bytes 4718596 | tf_op jit(solution)/shard_map/cond
  746.3 139.3 %copy-start.156 = (f32[1152]{0:T(1024)}, f32[1152]{0:T(1024)S(1)}, u32[]{:S(2)}) copy-start(f32[1152]{0:T(1024)S(1)} %get-tuple-element.1703) | copy-start | bytes 13828
  746.3 139.3 %copy-start.158 = (f32[1536]{0:T(1024)}, f32[1536]{0:T(1024)S(1)}, u32[]{:S(2)}) copy-start(f32[1536]{0:T(1024)S(1)} %get-tuple-element.1721) | copy-start | bytes 18436
  746.3 139.3 %copy-start.177 = (f32[384]{0:T(512)}, f32[384]{0:T(512)S(1)}, u32[]{:S(2)}) copy-start(f32[384]{0:T(512)S(1)} %get-tuple-element.1709) | copy-start | bytes 4612
  746.3 139.3 %copy-start.179 = (f32[384]{0:T(512)}, f32[384]{0:T(512)S(1)}, u32[]{:S(2)}) copy-start(f32[384]{0:T(512)S(1)} %get-tuple-element.1712) | copy-start | bytes 4612
  746.3 139.3 %copy-start.181 = (f32[384]{0:T(512)}, f32[384]{0:T(512)S(1)}, u32[]{:S(2)}) copy-start(f32[384]{0:T(512)S(1)} %get-tuple-element.1715) | copy-start | bytes 4612
  746.3 139.2 %collective-permute-start.3 = (bf16[1,1024,384]{2,1,0:T(8,128)(2,1)}, bf16[1,1024,384]{2,1,0:T(8,128)(2,1)S(1)}, u32[]{:S(2)}, u32[]{:S(2)}) collective-permute-start(bf16[1,1024,384]{2,1,0:T(8,128)(2,1)} %get-tuple-element.1697), channel_id=1, source_target_pairs={{16,0},{17,1},{18,2},{19,3},{20,4},{21,5},{22,6},{23,7},{24,8},{25... | collective-permute-start | bytes 2359304 | tf_op jit(solution)/shard_map/ppermute | solution.py:19
  917.1 14.6 %copy-start.21 = (f32[1024,384]{1,0:T(8,128)}, f32[1024,384]{1,0:T(8,128)S(1)}, u32[]{:S(2)}) copy-start(f32[1024,384]{1,0:T(8,128)S(1)} %get-tuple-element.2786) | copy-start | bytes 4718596 | tf_op jit(solution)/shard_map/cond
  1225.2 80.7 %copy-start.106 = (bf16[1,2,1,1024,384]{4,3,2,1,0:T(8,128)(2,1)}, bf16[1,2,1,1024,384]{4,3,2,1,0:T(8,128)(2,1)S(1)}, u32[]{:S(2)}) copy-start(bf16[1,2,1,1024,384]{4,3,2,1,0:T(8,128)(2,1)S(1)} %bitcast_dynamic-update-slice_fusion.4) | copy-start | bytes 4718596
  (126 other events, 513.7 us)
Sparse Core Ops, SparseCore 0:
  1150.0 152.0 all-reduce.3
where the time goes:
time: 1340 us; the launch traced here: 1320 us
  waiting for transfers between devices  454 us (34%)
  local copies, waits for them, and re-layouts  362 us (27%)
  matrix products  210 us (16%)
  other arithmetic  179 us (13%)
  blocking collectives  63.4 us (5%)
  loops' own time  21.7 us (2%)
  between operations  15.5 us (1%)
    ppermute x4, waiting for transfers between devices, shifted(): lax.ppermute(value, axis, [(source, source + steps) for source in range(f...  377 us
    psum x1, waiting for transfers between devices, body(): lax.psum((totals[0], totals[1], totals[2], totals[3], totals[4], totals[5...  76.9 us
    rev x8, local copies, waits for them, and re-layouts, partner(): return value.reshape(count, -1, 2)[:, :, ::-1].reshape(count, -1)  65.7 us
    another operation x64, local copies, waits for them, and re-layouts  65.6 us
    psum x1, blocking collectives, body(): lax.psum((totals[0], totals[1], totals[2], totals[3], totals[4], totals[5...  63.4 us
    dynamic_update_slice x8, local copies, waits for them, and re-layouts, one_row(): lax.scan(one_block, (empty, empty), (q_row, dc_row, total_row, segq_row,...  63 us
    mul x2, other arithmetic, turn_back(): return grad * cosine + partner(grad * sine_signed)  48.4 us
    dot_general x2, matrix products, forward_layer(): jnp.dot(hidden_low, w_up, preferred_element_type=jnp.float32) + b_up  36.1 us
  transfers between devices with their start and end apart: 5, of which 4 were waited for; matrix products, arithmetic and copies ran while one was open for 3% of the time, Pallas kernels for 0%

commit v1 on v0

v1 whole, which is shorter than its diff:
```python
import functools

import jax
import jax.numpy as jnp
import ml_dtypes
import numpy as np
from jax import lax
from jax.experimental import pallas as pl
from jax.experimental.pallas import tpu as pltpu
from jax.sharding import PartitionSpec as P

HEAD_DIM = 64
LANES = 128
HALO = 64
BLOCK = 128
WINDOW = BLOCK + 2 * HALO
CHUNK = 256
TILE = 512
NEG_LARGE = -1e30
NORM_EPS = 1e-12
MESH = pl.DeviceIdType.MESH
BF = jnp.bfloat16
F32 = jnp.float32


def rotary_rows():
    place = np.arange(HALO, dtype=np.float64)[:, None]
    lane = np.arange(LANES)
    angle = place * 10000.0 ** (-2.0 * (lane % 32) / HEAD_DIM)
    sign = np.where(lane < HALO, -1.0, 1.0)
    exact = np.concatenate([np.cos(angle), np.sin(angle) * sign], axis=1).astype(np.float32)
    high = exact.astype(ml_dtypes.bfloat16)
    low = (exact - high.astype(np.float32)).astype(ml_dtypes.bfloat16)
    return np.concatenate([high, low], axis=0)


def dot(a, b):
    return lax.dot_general(a, b, (((1,), (0,)), ((), ())), preferred_element_type=F32)


def dot_t(a, b):
    return lax.dot_general(a, b, (((1,), (1,)), ((), ())), preferred_element_type=F32)


def t_dot(a, b):
    return lax.dot_general(a, b, (((0,), (0,)), ((), ())), preferred_element_type=F32)


def fold(v):
    return jnp.sum(v.reshape(v.shape[0] // 8, 8, v.shape[1]), axis=0)


def mean(v):
    return jnp.sum(v, axis=-1, keepdims=True) * (1.0 / v.shape[-1])


def standard(v):
    centred = v - mean(v)
    rstd = lax.rsqrt(mean(centred * centred) + NORM_EPS)
    return centred * rstd, rstd


def norm_back(weighted, hat, rstd):
    return rstd * (weighted - mean(weighted) - hat * mean(weighted * hat))


def pair_order(shape):
    row = lax.broadcasted_iota(jnp.int32, shape, 0)
    lane = lax.broadcasted_iota(jnp.int32, shape, 1)
    rest = lane % 64
    return (row == (rest // 32) * 64 + (rest % 32) * 2 + lane // 64).astype(F32).astype(BF)


def kernel(
    tokens, segs, cot, w_qkv, b_qkv, w_out, b_out, gain1, bias1, w_up, b_up, w_down, b_down, gain2, bias2, table,
    layer_out, in_grad, g_qkv, g_out, g_up, g_down, g_small,
    X, E, QKV, PT, CTX, HID, ACT, SL, HAT1, HAT2, R1, R2, COS, SIN, SEG, BK1, DC, CARRY,
    WQKV, WOUT, WUP, WDOWN, BQKV, LO, IG, TB, GT, SUMS,
    load_sem, x_sem, out_sem, send_f, recv_f, send_b, recv_b, grad_sem,
):
    micros, _, length, width = tokens.shape
    ff = w_up.shape[2]
    chunks = length // CHUNK
    per_chunk = CHUNK // BLOCK
    pairs = width // LANES
    sec = lax.axis_index("section")
    first = sec == 0
    other = {"section": 1 - sec}

    loads = [
        pltpu.make_async_copy(src.at[0], dst, load_sem.at[i])
        for i, (src, dst) in enumerate([(w_qkv, WQKV), (w_out, WOUT), (w_up, WUP), (w_down, WDOWN)])
    ]
    for copy in loads:
        copy.start()

    def own_rows(m):
        return (
            pltpu.make_async_copy(tokens.at[m, 0], X.at[m], x_sem.at[m]),
            pltpu.make_async_copy(cot.at[m, 0], E.at[m], x_sem.at[m]),
        )

    for m in range(micros):

        @pl.when(first)
        def _(m=m):
            own_rows(m)[0].start()

        @pl.when(jnp.logical_not(first))
        def _(m=m):
            own_rows(m)[1].start()

    barrier = pltpu.get_barrier_semaphore()
    pl.semaphore_signal(barrier, inc=1, device_id=other, device_id_type=MESH)
    pl.semaphore_wait(barrier, 1)

    def rows(c):
        return pl.ds(pl.multiple_of(c * CHUNK, CHUNK), CHUNK)

    def padded(c):
        return pl.ds(pl.multiple_of(c * CHUNK + HALO, HALO), CHUNK)

    def send_forward(m, c):
        return pltpu.make_async_remote_copy(
            src_ref=LO.at[m, rows(c), :], dst_ref=X.at[m, rows(c), :],
            send_sem=send_f.at[m, c], recv_sem=recv_f.at[m, c],
            device_id=other, device_id_type=MESH,
        )

    def send_backward(m, c):
        return pltpu.make_async_remote_copy(
            src_ref=IG.at[m, rows(c), :], dst_ref=E.at[m, rows(c), :],
            send_sem=send_b.at[m, c], recv_sem=recv_b.at[m, c],
            device_id=other, device_id_type=MESH,
        )

    def keep_out(m, c):
        return pltpu.make_async_copy(LO.at[m, rows(c), :], layer_out.at[0, m, 0, rows(c), :], out_sem.at[0, m, c])

    def keep_in(m, c):
        return pltpu.make_async_copy(IG.at[m, rows(c), :], in_grad.at[0, m, 0, rows(c), :], out_sem.at[1, m, c])

    lane_row = lax.broadcasted_iota(jnp.int32, (BLOCK, LANES), 1)
    token_row = lax.broadcasted_iota(jnp.int32, (BLOCK, LANES), 0)
    for m in range(micros):
        edge = jnp.full((HALO, LANES), -1.0, F32)
        SEG[m, :HALO, :] = edge
        SEG[m, length + HALO :, :] = edge
        for ref in (COS, SIN):
            ref[m, :HALO, :] = jnp.zeros((HALO, LANES), F32)
            ref[m, length + HALO :, :] = jnp.zeros((HALO, LANES), F32)
        blank = jnp.zeros((HALO, 3 * width), BF)
        QKV[m, :HALO, :] = blank
        QKV[m, length + HALO :, :] = blank
        for b in range(length // BLOCK):
            own = segs[m, :, b * BLOCK : (b + 1) * BLOCK].astype(F32)
            column = jnp.broadcast_to(own, (BLOCK, LANES)).T
            SEG[m, HALO + b * BLOCK : HALO + (b + 1) * BLOCK, :] = column
            ahead = (column == own) & (lane_row < token_row)
            count = ahead.astype(F32)
            if b:
                before = segs[m, :, (b - 1) * BLOCK : b * BLOCK].astype(F32)
                count += (column == before).astype(F32)
            place = jnp.sum(count, axis=-1, keepdims=True)
            pick = (place == (lane_row % HALO).astype(F32)).astype(F32).astype(BF)
            values = dot(pick, table[...])
            COS[m, HALO + b * BLOCK : HALO + (b + 1) * BLOCK, :] = values[:, :LANES]
            SIN[m, HALO + b * BLOCK : HALO + (b + 1) * BLOCK, :] = values[:, LANES:]
    SUMS[...] = jnp.zeros_like(SUMS)

    order = pair_order((LANES, LANES))
    loads[0].wait()
    BQKV[...] = jnp.broadcast_to(b_qkv[...].astype(F32), BQKV.shape)
    for j in range(2 * pairs):
        cols = slice(j * LANES, (j + 1) * LANES)
        WQKV[:, cols] = dot(WQKV[:, cols], order).astype(BF)
        BQKV[:, cols] = dot(BQKV[:, cols].astype(BF), order)
    for copy in loads[1:]:
        copy.wait()

    lane = lax.broadcasted_iota(jnp.int32, (BLOCK, LANES), 1)
    first_turned = lane % 64 < 32
    first_plain = lane < 64
    zero = jnp.zeros((BLOCK, LANES), BF)

    def two_heads(v, is_first):
        return jnp.concatenate([jnp.where(is_first, v, zero), jnp.where(is_first, zero, v)], axis=0)

    def f_qkv(m, c):
        x = X[m, rows(c), :]
        cosine, sine = COS[m, padded(c), :], SIN[m, padded(c), :]
        for g in range(3):
            cols = slice(g * width, (g + 1) * width)
            y = dot(x, WQKV[:, cols]) + BQKV[:1, cols]
            for j in range(pairs):
                v = y[:, j * LANES : (j + 1) * LANES]
                if g < 2:
                    v = v * cosine + pltpu.roll(v, 64, 1) * sine
                if g == 0:
                    v = v * HEAD_DIM**-0.5
                QKV[m, padded(c), g * width + j * LANES : g * width + (j + 1) * LANES] = v.astype(BF)

    def window(b):
        return pl.ds(pl.multiple_of(b * BLOCK, BLOCK), WINDOW)

    def queries(b):
        return pl.ds(pl.multiple_of(b * BLOCK + HALO, HALO), BLOCK)

    def f_attn(m, b):
        own = segs[m, :, pl.ds(pl.multiple_of(b * BLOCK, BLOCK), BLOCK)].astype(F32)
        shut = jnp.where(SEG[m, window(b), :] == own, 0.0, NEG_LARGE)
        shut = jnp.concatenate([shut, shut], axis=1)
        for j in range(pairs):
            q = QKV[m, queries(b), j * LANES : (j + 1) * LANES]
            k = QKV[m, window(b), width + j * LANES : width + (j + 1) * LANES]
            v = QKV[m, window(b), 2 * width + j * LANES : 2 * width + (j + 1) * LANES]
            score = dot_t(k, two_heads(q, first_turned)) + shut
            raised = jnp.exp(score - jnp.max(score, axis=0, keepdims=True))
            probs = (raised * (1.0 / jnp.sum(raised, axis=0, keepdims=True))).astype(BF)
            PT[m, b, j] = probs
            mixed = t_dot(v, probs)
            turned = jnp.concatenate([mixed[:64, :BLOCK], mixed[64:, BLOCK:]], axis=0)
            CTX[m, pl.ds(pl.multiple_of(b * BLOCK, BLOCK), BLOCK), j * LANES : (j + 1) * LANES] = turned.T.astype(BF)

    def f_rest(m, c):
        r = rows(c)
        h = X[m, r, :].astype(F32) + dot(CTX[m, r, :], WOUT[...]) + b_out[...].astype(F32)
        hat, rstd = standard(h)
        HAT1[m, r, :] = hat.astype(BF)
        R1[m, r, :] = jnp.broadcast_to(rstd, (CHUNK, LANES))
        hidden = hat * gain1[...].astype(F32) + bias1[...].astype(F32)
        low = hidden.astype(BF)
        HID[m, r, :] = low
        for n in range(0, ff, TILE):
            cols = slice(n, n + TILE)
            u = dot(low, WUP[:, cols]) + b_up[:, cols].astype(F32)
            cdf = 0.5 * lax.erf(u * 0.7071067811865476) + 0.5
            ACT[m, r, cols] = (u * cdf).astype(BF)
            SL[m, r, cols] = (cdf + u * (jnp.exp(u * u * -0.5) * 0.3989422804014327)).astype(BF)
        hat, rstd = standard(hidden + dot(ACT[m, r, :], WDOWN[...]) + b_down[...].astype(F32))
        HAT2[m, r, :] = hat.astype(BF)
        R2[m, r, :] = jnp.broadcast_to(rstd, (CHUNK, LANES))
        LO[m, r, :] = (hat * gain2[...].astype(F32) + bias2[...].astype(F32)).astype(BF)

    wide = 3 * width
    at = {}
    spot = 0
    for name, size in [("qkv", wide), ("out", width), ("gain1", width), ("bias1", width), ("up", ff), ("down", width), ("gain2", width), ("bias2", width)]:
        at[name] = slice(spot, spot + size)
        spot += size

    def add(name, v, cols=None):
        place = at[name]
        if cols is not None:
            place = slice(place.start + cols.start, place.start + cols.stop)
        SUMS[:, place] += fold(v)

    def spread(v):
        return jnp.concatenate([v] * pairs, axis=1)

    def b_ffn(m, c):
        r = rows(c)
        e = E[m, r, :].astype(F32)
        hat = HAT2[m, r, :].astype(F32)
        add("gain2", e * hat)
        add("bias2", e)
        back2 = norm_back(e * gain2[...].astype(F32), hat, spread(R2[m, r, :]))
        down = back2.astype(BF)
        E[m, r, :] = down
        add("down", down.astype(F32))
        for n in range(0, ff, TILE):
            cols = slice(n, n + TILE)
            up = (dot_t(down, WDOWN[cols, :]) * SL[m, r, cols].astype(F32)).astype(BF)
            SL[m, r, cols] = up
            add("up", up.astype(F32), cols)
        d_hidden = back2 + dot_t(SL[m, r, :], WUP[...])
        hat = HAT1[m, r, :].astype(F32)
        add("gain1", d_hidden * hat)
        add("bias1", d_hidden)
        back1 = norm_back(d_hidden * gain1[...].astype(F32), hat, spread(R1[m, r, :]))
        BK1[r, :] = back1
        mixed = back1.astype(BF)
        HAT1[m, r, :] = mixed
        add("out", mixed.astype(F32))
        DC[...] = dot_t(mixed, WOUT[...]).astype(BF)

    def turn_back(v, cosine, sine):
        return v * cosine - pltpu.roll(v, 64, 1) * sine

    def b_attn(m, b, i):
        cosine, sine = COS[m, queries(b), :], SIN[m, queries(b), :]
        done = pl.ds(pl.multiple_of(b * BLOCK, BLOCK), BLOCK)
        cosine_k, sine_k = COS[m, done, :], SIN[m, done, :]
        for j in range(pairs):
            cols = slice(j * LANES, (j + 1) * LANES)
            q = two_heads(QKV[m, queries(b), cols], first_turned)
            k = QKV[m, window(b), width + j * LANES : width + (j + 1) * LANES]
            v = QKV[m, window(b), 2 * width + j * LANES : 2 * width + (j + 1) * LANES]
            dc = two_heads(DC[i * BLOCK : (i + 1) * BLOCK, cols], first_plain)
            probs = PT[m, b, j]
            part = probs.astype(F32)
            weighted = part * dot_t(v, dc)
            score = (weighted - part * jnp.sum(weighted, axis=0, keepdims=True)).astype(BF)
            dq = t_dot(k, score)
            dq = jnp.concatenate(
                [dq[:32, :BLOCK], dq[32:64, BLOCK:], dq[64:96, :BLOCK], dq[96:, BLOCK:]], axis=0
            ).T * HEAD_DIM**-0.5
            dk = dot(score, q)
            dv = dot(probs, dc)
            QKV[m, queries(b), cols] = turn_back(dq, cosine, sine).astype(BF)
            kept_k, kept_v = CARRY[:, cols], CARRY[:, width + j * LANES : width + (j + 1) * LANES]
            QKV[m, done, width + j * LANES : width + (j + 1) * LANES] = turn_back(
                dk[:BLOCK] + kept_k, cosine_k, sine_k
            ).astype(BF)
            QKV[m, done, 2 * width + j * LANES : 2 * width + (j + 1) * LANES] = (dv[:BLOCK] + kept_v).astype(BF)
            CARRY[:, cols] = dk[BLOCK:]
            CARRY[:, width + j * LANES : width + (j + 1) * LANES] = dv[BLOCK:]

    def b_flush(m):
        last = slice(length, length + HALO)
        for j in range(pairs):
            cols = slice(j * LANES, (j + 1) * LANES)
            QKV[m, last, width + j * LANES : width + (j + 1) * LANES] = turn_back(
                CARRY[:HALO, cols], COS[m, last, :], SIN[m, last, :]
            ).astype(BF)
            QKV[m, last, 2 * width + j * LANES : 2 * width + (j + 1) * LANES] = CARRY[
                :HALO, width + j * LANES : width + (j + 1) * LANES
            ].astype(BF)

    def b_in(m, c):
        d_proj = QKV[m, padded(c), :]
        add("qkv", d_proj.astype(F32))
        IG[m, rows(c), :] = (BK1[rows(c), :] + dot_t(d_proj, WQKV[...])).astype(BF)

    def forward(m):
        @pl.when(first)
        def _():
            own_rows(m)[0].wait()

        def arrive(c):
            @pl.when(jnp.logical_not(first))
            def _():
                send_forward(m, c).wait_recv()

        arrive(0)
        f_qkv(m, 0)

        def step(c, carry):
            @pl.when(c + 1 < chunks)
            def _():
                arrive(c + 1)
                f_qkv(m, c + 1)

            for i in range(per_chunk):
                f_attn(m, c * per_chunk + i)
            f_rest(m, c)
            keep_out(m, c).start()

            @pl.when(first)
            def _():
                send_forward(m, c).start()

            return carry

        lax.fori_loop(0, chunks, step, 0)

    def backward(m):
        @pl.when(jnp.logical_not(first))
        def _():
            own_rows(m)[1].wait()

        CARRY[...] = jnp.zeros_like(CARRY)

        def leave(c):
            b_in(m, c)
            keep_in(m, c).start()

            @pl.when(jnp.logical_not(first))
            def _():
                send_backward(m, c).start()

        def step(c, carry):
            @pl.when(first)
            def _():
                send_backward(m, c).wait_recv()

            b_ffn(m, c)
            for i in range(per_chunk):
                b_attn(m, c * per_chunk + i, i)

            @pl.when(c > 0)
            def _():
                leave(c - 1)

            return carry

        lax.fori_loop(0, chunks, step, 0)
        b_flush(m)
        leave(chunks - 1)

    def phase(step, carry):
        m = jnp.where(first, step % 2, step // 2)
        turn = jnp.where(first, step // 2, step % 2)

        @pl.when(turn == 0)
        def _():
            forward(m)

        @pl.when(turn == 1)
        def _():
            backward(m)

        return carry

    lax.fori_loop(0, 2 * micros, phase, 0)

    def turned(ref):
        for m in range(micros):
            TB[:, m * length : (m + 1) * length] = ref[m].T

    def total(ref, cols, shift=0):
        return sum(
            dot(TB[:, m * length : (m + 1) * length], ref[m, shift : shift + length, cols]) for m in range(micros)
        )

    turned(E)
    for n in range(0, ff, TILE):
        GT[n : n + TILE, :width] = total(ACT, slice(n, n + TILE)).T
    store_down = pltpu.make_async_copy(GT.at[:, pl.ds(0, width)], g_down.at[0], grad_sem.at[0])
    store_down.start()
    turned(HID)
    store_down.wait()
    for n in range(0, ff, TILE):
        LOW = total(SL, slice(n, n + TILE))
        GT[n : n + width, :TILE] = LOW
    stores = [
        pltpu.make_async_copy(GT.at[pl.ds(n, width), pl.ds(0, TILE)], g_up.at[0, :, pl.ds(n, TILE)], grad_sem.at[1 + i])
        for i, n in enumerate(range(0, ff, TILE))
    ]
    for s in stores:
        s.start()
    turned(CTX)
    for s in stores:
        s.wait()
    GT[:width, :width] = total(HAT1, slice(0, width))
    turned(X)
    for g in range(3):
        part = total(QKV, slice(g * width, (g + 1) * width), HALO)
        if g < 2:
            part = jnp.concatenate(
                [dot_t(part[:, j * LANES : (j + 1) * LANES].astype(BF), order) for j in range(pairs)], axis=1
            )
        GT[(g + 1) * width : (g + 2) * width, :width] = part
    stores = [pltpu.make_async_copy(GT.at[pl.ds(0, width), pl.ds(0, width)], g_out.at[0], grad_sem.at[0])]
    stores += [
        pltpu.make_async_copy(
            GT.at[pl.ds((g + 1) * width, width), pl.ds(0, width)], g_qkv.at[0, :, pl.ds(g * width, width)], grad_sem.at[1 + g]
        )
        for g in range(3)
    ]
    for s in stores:
        s.start()
    small = jnp.sum(SUMS[...], axis=0, keepdims=True)
    g_small[...] = small
    high = jnp.broadcast_to(small[:, : 2 * width], (16, 2 * width))
    for j in range(2 * pairs):
        cols = slice(j * LANES, (j + 1) * LANES)
        top = high[:, cols].astype(BF)
        rest = (high[:, cols] - top.astype(F32)).astype(BF)
        g_small[:, cols] = (dot_t(top, order) + dot_t(rest, order))[:1]
    for s in stores:
        s.wait()

    def finish(i, carry):
        m, c = i // chunks, i % chunks
        keep_out(m, c).wait()
        keep_in(m, c).wait()

        @pl.when(first)
        def _():
            send_forward(m, c).wait_send()

        @pl.when(jnp.logical_not(first))
        def _():
            send_backward(m, c).wait_send()

        return carry

    lax.fori_loop(0, micros * chunks, finish, 0)


def body(tokens, segments, cotangent, *params):
    micros, _, length, width = tokens.shape
    ff = params[6].shape[2]
    chunks, blocks, pairs = length // CHUNK, length // BLOCK, width // LANES
    small = 3 * width + 6 * width + ff
    any_space, vmem = pl.BlockSpec(memory_space=pl.ANY), pl.BlockSpec(memory_space=pltpu.VMEM)
    big = {0, 3, 5, 9, 11}
    specs = [any_space, vmem, any_space]
    specs += [any_space if i in (0, 2, 6, 8) else vmem for i in range(12)] + [vmem]
    table = jnp.asarray(rotary_rows())

    def scratch(*shape, dtype=BF):
        return pltpu.VMEM(shape, dtype)

    row = (micros, length, width)
    scratches = [
        scratch(*row), scratch(*row), scratch(micros, length + 2 * HALO, 3 * width),
        scratch(micros, blocks, pairs, WINDOW, 2 * BLOCK), scratch(*row), scratch(*row),
        scratch(micros, length, ff), scratch(micros, length, ff), scratch(*row), scratch(*row),
        scratch(micros, length, LANES, dtype=F32), scratch(micros, length, LANES, dtype=F32),
        scratch(micros, length + 2 * HALO, LANES, dtype=F32), scratch(micros, length + 2 * HALO, LANES, dtype=F32),
        scratch(micros, length + 2 * HALO, LANES, dtype=F32),
        scratch(length, width, dtype=F32), scratch(CHUNK, width), scratch(BLOCK, 2 * width, dtype=F32),
        scratch(width, 3 * width), scratch(width, width), scratch(width, ff), scratch(ff, width),
        scratch(16, 3 * width, dtype=F32), scratch(*row), scratch(*row),
        scratch(width, micros * length), scratch(ff, TILE, dtype=F32), scratch(8, small, dtype=F32),
        pltpu.SemaphoreType.DMA((4,)), pltpu.SemaphoreType.DMA((micros,)), pltpu.SemaphoreType.DMA((2, micros, chunks)),
        pltpu.SemaphoreType.DMA((micros, chunks)), pltpu.SemaphoreType.DMA((micros, chunks)),
        pltpu.SemaphoreType.DMA((micros, chunks)), pltpu.SemaphoreType.DMA((micros, chunks)),
        pltpu.SemaphoreType.DMA((4,)),
    ]
    S = jax.ShapeDtypeStruct
    outs = (
        S((1,) + tokens.shape, BF), S((1,) + tokens.shape, BF),
        S((1, width, 3 * width), F32), S((1, width, width), F32), S((1, width, ff), F32), S((1, ff, width), F32),
        S((1, small), F32),
    )
    layer_out, in_grad, g_qkv, g_out, g_up, g_down, g_small = pl.pallas_call(
        kernel,
        out_shape=outs,
        in_specs=specs,
        out_specs=(any_space,) * 6 + (vmem,),
        scratch_shapes=scratches,
        compiler_params=pltpu.CompilerParams(
            collective_id=0, has_side_effects=True, vmem_limit_bytes=64 * 1024 * 1024
        ),
        name="relay",
    )(tokens, segments, cotangent, *params, table)
    g_qkv, g_out, g_up, g_down, g_small = lax.psum((g_qkv, g_out, g_up, g_down, g_small), "batch")
    sizes = [3 * width, width, width, width, ff, width, width, width]
    ends = np.cumsum(sizes)
    s_qkv, s_out, s_gain1, s_bias1, s_up, s_down, s_gain2, s_bias2 = (
        g_small[:, e - n : e] for e, n in zip(ends, sizes)
    )
    return (
        layer_out, in_grad, g_qkv, s_qkv, g_out, s_out, s_gain1, s_bias1,
        g_up, s_up, g_down, s_down, s_gain2, s_bias2,
    )


def solution(mesh):
    rows, ids = P(None, "batch", None, None), P(None, "batch", None)
    matrix, vector = P("section", None, None), P("section", None)
    weights = (matrix, vector, matrix, vector, vector, vector, matrix, vector, matrix, vector, vector, vector)
    kept = P("section", None, "batch", None, None)
    return jax.shard_map(
        body,
        mesh=mesh,
        in_specs=(rows, ids, rows) + weights,
        out_specs=(kept, kept) + weights,
        check_vma=False,
    )
```

time: 1340 us -> 308 us (0.23); the launches traced: 1320 us -> 308 us
  waiting for transfers between devices: 454 us -> 88.8 us
  local copies, waits for them, and re-layouts: 362 us -> 12.2 us
  matrix products: 210 us -> 0 us
  other arithmetic: 179 us -> 0 us
  Pallas kernels: 0 us -> 131 us
  loops' own time: 21.7 us -> 0 us
    ppermute x4 -> x0, waiting for transfers between devices: 377 us -> none  [shifted(): lax.ppermute(value, axis, [(source, source + steps) for source in range(f...]
    dot_general x52 -> x0, matrix products: 210 us -> none  [the longest x2 36.1 us: forward_layer(): jnp.dot(hidden_low, w_up, preferred_element_type=jnp.float32) + b_up]
    pallas_call x0 -> x1, Pallas kernels: none -> 131 us  [body(): pl.pallas_call(kernel, out_shape=outs, in_specs=specs, out_specs=(any_spa...]
    dynamic_update_slice x16 -> x0, local copies, waits for them, and re-layouts: 87.9 us -> none  [the longest x8 63 us: one_row(): lax.scan(one_block, (empty, empty), (q_row, dc_row, total_row, segq_row,...]
    rev x8 -> x0, local copies, waits for them, and re-layouts: 65.7 us -> none  [partner(): return value.reshape(count, -1, 2)[:, :, ::-1].reshape(count, -1)]
    another operation x64 -> x0, local copies, waits for them, and re-layouts: 65.6 us -> none
    mul x6 -> x0, other arithmetic: 48.4 us -> none  [the longest x2 48.4 us: turn_back(): return grad * cosine + partner(grad * sine_signed)]
    reshape x20 -> x0, local copies, waits for them, and re-layouts: 39.9 us -> none  [the longest x16 27.1 us: partner(): return value.reshape(count, -1, 2)[:, :, ::-1].reshape(count, -1)]
  transfers between devices with their start and end apart: 5 -> 1, of which waited for: 4 -> 1; matrix products, arithmetic and copies ran while one was open for 3% -> 1% of each run, Pallas kernels for 0% -> 0%
where the time goes in v1:
time: 308 us
  Pallas kernels  131 us (43%)
  waiting for transfers between devices  88.8 us (29%)
  blocking collectives  61.2 us (20%)
  between operations  14.1 us (5%)
  local copies, waits for them, and re-layouts  12.2 us (4%)
    pallas_call x1, Pallas kernels, body(): pl.pallas_call(kernel, out_shape=outs, in_specs=specs, out_specs=(any_spa...  131 us
    psum x1, waiting for transfers between devices, body(): lax.psum((g_qkv, g_out, g_up, g_down, g_small), 'batch')  88.7 us
    psum x1, blocking collectives, body(): lax.psum((g_qkv, g_out, g_up, g_down, g_small), 'batch')  61.2 us
    unnamed x20, local copies, waits for them, and re-layouts  10.5 us
  transfers between devices with their start and end apart: 1, of which 1 were waited for; matrix products, arithmetic and copies ran while one was open for 1% of the time, Pallas kernels for 0%

profile of v1, /device:TPU:0, one launch (start us, length us, event | category | flops | bytes accessed | tf_op | source)
XLA Modules:
  0.0 307.7 jit_solution(13997150577629508558)
XLA Ops:
  7.2 0.0 all-reduce.3.cloned.1.call-start
  7.2 131.4 %relay.1 = (bf16[1,2,1,1024,384]{4,3,2,1,0:T(8,128)(2,1)}, bf16[1,2,1,1024,384]{4,3,2,1,0:T(8,128)(2,1)}, f32[1,384,1152]{2,1,0:T(8,128)}, f32[1,384,384]{2,1,0:...) custom-call(bf16[2,1,1024,384]{3,2,1,0:T(8,128)(2,1)} %tokens.1, ...), custom_call_target="tpu_custom_call" | custom-call | tf_op jit(solution)/shard_map/relay/pallas_call | solution.py:529
  138.6 0.0 copy-start.6
  138.6 0.0 copy-start.4
  138.6 0.0 all-reduce.3.cloned.1.call-update
  138.6 0.0 copy-start.3
  138.7 0.7 copy-done.6
  139.3 61.2 %psum.36 = f32[1,4992]{1,0:T(1,128)S(1)} all-reduce(f32[1,4992]{1,0:T(1,128)S(1)} %copy-done.6), channel_id=1, replica_groups=mesh['section'=2,'batch'=16] {'batch'}, use_global_device_ids=true, to_apply=%region_1.0 | all-reduce | flops 4992 | bytes 39936 | tf_op jit(solution)/shard_map/psum | solution.py:540
  200.5 0.6 slice.32
  201.1 0.6 slice.36
  201.7 0.6 fusion
  202.3 88.7 %all-reduce.3.cloned.1.call-done = (f32[1,384,1152]{2,1,0:T(8,128)}, f32[1,384,384]{2,1,0:T(8,128)}, f32[1,384,1536]{2,1,0:T(8,128)}, f32[1,1536,384]{2,1,0:T(8,128)}) async-done(((f32[1,384,1152]{2,1,0:T(8,128)}, f32[1,384,384]{2,1,0:T(8,128)}, f32[1,384,1536]{2,1,0:T(8,128)}, f32[1,1536,384]{2,1,0:T(8,128)}), (f32[1,384,1152]{2,1,0:T(8,128)}, f32[1,384,384]{2,1,0:T(8,128)}, f32[1,384,1536]{2,1,0:T(8,128)}, ...) | async-done | bytes 7077904 | tf_op jit(solution)/shard_map/psum | solution.py:540
  291.0 0.0 copy-done.4
  291.0 1.1 copy.40
  292.2 0.0 copy-done.3
  292.2 0.0 copy-start.2
  292.2 1.1 copy.41
  293.3 0.9 copy-done.2
  294.2 0.0 copy-start.5
  294.2 0.0 copy-start.1
  294.2 1.2 copy.42
  295.4 0.2 copy-done.5
  295.7 0.8 copy.43
  296.5 0.4 copy-done.1
  296.9 0.0 copy-start
  296.9 1.4 copy.44
  298.3 1.1 copy-done
  299.4 1.4 copy.45
Async XLA Ops:
  7.2 283.8 %all-reduce.3.cloned.1.call-start = ((), (), s32[]{:S(2)}) async-start(), calls=%async_computation | async-start | bytes 14155776 | tf_op jit(solution)/shard_map/psum | solution.py:540
  138.6 0.7 copy-start.6
  138.6 152.4 %copy-start.4 = (bf16[1,2,1,1024,384]{4,3,2,1,0:T(8,128)(2,1)S(1)}, bf16[1,2,1,1024,384]{4,3,2,1,0:T(8,128)(2,1)}, u32[]{:S(2)}) copy-start(bf16[1,2,1,1024,384]{4,3,2,1,0:T(8,128)(2,1)} %get-tuple-element.52) | copy-start | bytes 4718596
  138.6 153.5 %copy-start.3 = (bf16[1,2,1,1024,384]{4,3,2,1,0:T(8,128)(2,1)S(1)}, bf16[1,2,1,1024,384]{4,3,2,1,0:T(8,128)(2,1)}, u32[]{:S(2)}) copy-start(bf16[1,2,1,1024,384]{4,3,2,1,0:T(8,128)(2,1)} %get-tuple-element.53) | copy-start | bytes 4718596
  292.2 2.0 copy-start.2
  294.2 1.4 copy-start.5
  294.2 2.7 copy-start.1
  296.9 2.5 copy-start
Sparse Core Ops, SparseCore 0:
  138.8 152.2 all-reduce.2
